TPU v7x, 512 devices: a whole 4x8x8 slice. The times are simulated.
512 devices in a mesh: rep: 16 (over y, x_lo), shard: 32 (over x_hi, z, core).
Axes of the slice: x: 4 (x_hi: 2, x_lo: 2; x = x_hi * 2 + x_lo), y: 8, z: 8, core: 2. Of those that a mesh axis runs over, the one named last changes fastest.
Arguments:
- pooled_cot: bfloat16 [32768, 32, 256], P(('rep', 'shard')), may hold values from -6 to 6
- bag_ids: int32 [32768, 32, 2], P('rep', 'shard'), may hold values from 0 to 3071, as said below
- table: bfloat16 [98304, 256], P('shard'), may hold values from -3 to 3
- accum: float32 [98304], P('shard'), may hold values from 0.5 to 8
- listed_block_index: int32 [16, 64], P('rep', 'shard'), may hold values from 0 to 23, as said below
- counts: int32 [16, 32], P('rep', 'shard'), may hold values from 1 to 2, as said below
- x_zero: bfloat16 [32768, 256], P(('rep', 'shard')), may hold values from -6 to 6
- w_top: bfloat16 [256, 2048], replicated, may hold values from -0.375 to 0.375
- u_proj: bfloat16 [256, 256], replicated, may hold values from -0.375 to 0.375
- v_proj: bfloat16 [256, 256], replicated, may hold values from -0.375 to 0.375
- cross_bias: float32 [256], replicated, may hold values from -3 to 3
- d_act: bfloat16 [32768, 2048], P(('rep', 'shard')), may hold values from -24 to 24
Outputs:
- new_table: bfloat16 [98304, 256], P('shard')
- new_accum: float32 [98304], P('shard')
- dense_grad: float32 [655360], P(('rep', 'shard'))
Inputs may be any that keep to these rules, and one draw needn't show every extreme that they name: `listed_block_index`: each device's first counts slots name distinct blocks of its slab, the remaining slots repeat arbitrary blocks. `counts`: live slots of each device; in every replica some device has all 2 live. `bag_ids`: every id lies in a block of a live slot of the device that owns its feature in its sample's replica.
All inputs are finite; a program needn't handle non-finite values.
Results may differ from a plain program's by a relative error of at most 0.0071.
Values may be sent and summed in bfloat16 or wider, within the bound.
A program may use at most 64 MiB of HBM per device.

v0:
```python
import jax
import jax.numpy as jnp
from jax import lax
from jax.sharding import PartitionSpec as P

BLOCK_ROWS = 128


learn_rate = 0.5


def on_device(
    pooled_cot,
    bag_ids,
    table,
    accum,
    listed_block_index,
    counts,
    x_zero,
    w_top,
    u_proj,
    v_proj,
    cross_bias,
    d_act,
):
    received = lax.all_to_all(pooled_cot, "shard", split_axis=1, concat_axis=0, tiled=True)
    embedding_width = table.shape[1]
    nblocks = table.shape[0] // BLOCK_ROWS
    slot_count = listed_block_index.shape[1]
    embedding_lookups = received.shape[0] * received.shape[1]
    pooled_rows = received.reshape(embedding_lookups, embedding_width)
    id_rows = bag_ids.reshape(embedding_lookups, bag_ids.shape[2])
    listed = listed_block_index[0]
    active_flags = jnp.arange(slot_count) < counts[0, 0]
    rows_per_slot = listed[:, None] * BLOCK_ROWS + jnp.arange(BLOCK_ROWS)[None, :]
    rows_per_slot = jnp.where(active_flags[:, None], rows_per_slot, -1).reshape(
        slot_count * BLOCK_ROWS, 1
    )
    lookup_hits = jnp.zeros((slot_count * BLOCK_ROWS, embedding_lookups), jnp.bfloat16)
    for pos in range(id_rows.shape[1]):
        lookup_hits = lookup_hits + (rows_per_slot == id_rows[None, :, pos]).astype(jnp.bfloat16)
    grad = jnp.dot(lookup_hits, pooled_rows, preferred_element_type=jnp.float32).reshape(
        slot_count, BLOCK_ROWS, embedding_width
    )
    slab = table.reshape(nblocks, BLOCK_ROWS, embedding_width)
    state = accum.reshape(nblocks, BLOCK_ROWS)
    old_rows = slab[listed]
    old_state = state[listed]
    acc_rows = old_state + jnp.mean(grad * grad, axis=2)
    new_rows = (
        old_rows.astype(jnp.float32) - learn_rate * grad * lax.rsqrt(acc_rows)[:, :, None]
    ).astype(jnp.bfloat16)
    masked = jnp.where(active_flags, listed, nblocks)
    replicas = lax.axis_size("rep")
    slab_rows = table.shape[0]
    picks = (masked[:, None] == jnp.arange(nblocks)[None, :]).astype(jnp.float32)
    row_change = new_rows.astype(jnp.float32) - old_rows.astype(jnp.float32)
    own_slab = jnp.einsum(
        "pb,pte->bte", picks, row_change, precision=lax.Precision.HIGHEST
    ).reshape(slab_rows, embedding_width)
    own_state = jnp.einsum(
        "pb,pt->bt", picks, acc_rows - old_state, precision=lax.Precision.HIGHEST
    ).reshape(slab_rows)
    slab_change, state_change = (
        lax.psum(own_slab.astype(jnp.bfloat16), "rep").astype(jnp.float32),
        lax.psum(own_state.astype(jnp.bfloat16), "rep").astype(jnp.float32),
    )
    new_table = (table.astype(jnp.float32) + slab_change / replicas).astype(jnp.bfloat16)
    new_accum = accum + state_change / replicas
    contract = (((0,), (0,)), ((), ()))
    hid = jnp.dot(x_zero, v_proj, preferred_element_type=jnp.float32).astype(jnp.bfloat16)
    mixed = (
        lax.dot_general(hid, u_proj, (((1,), (1,)), ((), ())), preferred_element_type=jnp.float32)
        + cross_bias
    )
    x_wide = x_zero.astype(jnp.float32)
    x_one = (x_wide * mixed + x_wide).astype(jnp.bfloat16)
    z_pre = jnp.dot(x_one, w_top, preferred_element_type=jnp.float32)
    sigma = jax.nn.sigmoid(z_pre)
    d_pre = (d_act.astype(jnp.float32) * sigma * (1.0 + z_pre * (1.0 - sigma))).astype(jnp.bfloat16)
    grad_w = lax.dot_general(d_pre, x_one, contract, preferred_element_type=jnp.float32)
    back_x = lax.dot_general(
        d_pre, w_top, (((1,), (1,)), ((), ())), preferred_element_type=jnp.float32
    )
    d_mix = (back_x * x_wide).astype(jnp.bfloat16)
    grad_u = lax.dot_general(d_mix, hid, contract, preferred_element_type=jnp.float32)
    d_hid = jnp.dot(d_mix, u_proj, preferred_element_type=jnp.float32).astype(jnp.bfloat16)
    grad_v = lax.dot_general(x_zero, d_hid, contract, preferred_element_type=jnp.float32)
    total = x_zero.shape[0] * replicas * lax.axis_size("shard")
    terms = jnp.concatenate([grad_w.ravel(), grad_u.ravel(), grad_v.ravel()]) * (
        1.0 / jnp.sqrt(jnp.float32(total))
    )
    dense_grad = lax.psum_scatter(terms, ("rep", "shard"), scatter_dimension=0, tiled=True)
    return (new_table, new_accum, dense_grad)


def solution(mesh):
    return jax.shard_map(
        on_device,
        mesh=mesh,
        in_specs=(
            P(("rep", "shard"), None, None),
            P("rep", "shard", None),
            P("shard", None),
            P("shard"),
            P("rep", "shard"),
            P("rep", "shard"),
            P(("rep", "shard"), None),
            P(),
            P(),
            P(),
            P(),
            P(("rep", "shard"), None),
        ),
        out_specs=(P("shard", None), P("shard"), P(("rep", "shard"))),
        check_vma=False,
    )
```

profile of v0, /device:TPU:1, one launch (start us, length us, event | category | flops | bytes accessed | tf_op | source)
XLA Modules:
  0.0 466.6 jit_solution(2565680718849697986)
XLA Ops:
  7.2 2.9 copy.21
  10.1 14.6 %all-to-all-start = ((bf16[64,32,256]{2,0,1:T(8,128)(2,1)}), bf16[64,32,256]{2,0,1:T(8,128)(2,1)}, u32[]{:S(2)}, u32[]{:S(2)}) async-start(bf16[64,32,256]{2,0,1:T(8,128)(2,1)} %copy.21), calls=%async_computation | async-start | bytes 2097152 | tf_op jit(solution)/shard_map/all_to_all | solution.py:26
  25.2 0.3 fusion.21
  25.5 1.9 convolution_bitcast_fusion
  27.3 0.5 fusion.2
  27.8 0.9 convolution_bitcast_fusion.2
  28.7 1.1 convolution_bitcast_fusion.1
  29.8 2.7 copy.25
  32.7 1.8 copy.24
  34.5 1.1 copy.27
  35.6 1.7 maximum_multiply_fusion
  38.2 0.6 gather_fusion.1
  38.8 0.6 gather_fusion
  39.4 13.1 %all-to-all-done = bf16[64,32,256]{2,0,1:T(8,128)(2,1)} async-done(((bf16[64,32,256]{2,0,1:T(8,128)(2,1)}), bf16[64,32,256]{2,0,1:T(8,128)(2,1)}, u32[]{:S(2)}, u32[]{:S(2)}) %all-to-all-start) | async-done | bytes 1048608 | tf_op jit(solution)/shard_map/all_to_all | solution.py:26
  52.5 1.9 multiply_reduce_fusion
  54.5 1.6 convolution_convert_fusion
  56.1 1.5 copy.23
  57.6 260.7 %all-reduce.6.cloned.1.call-done = f32[655360]{0:T(1024)} async-done(((f32[655360]{0:T(1024)}), f32[655360]{0:T(1024)}) %all-reduce.6.cloned.1.call-update) | async-done | bytes 2621456
  318.3 1.4 dynamic-slice
  319.7 0.3 fusion.4
  320.0 26.8 %psum.15 = bf16[3072]{0:T(1024)(128)(2,1)S(1)} all-reduce(bf16[3072]{0:T(1024)(128)(2,1)S(1)} %fusion.4), channel_id=1, replica_groups=mesh['rep'=16,'shard'=32] {'rep'}, use_global_device_ids=true, to_apply=%region_2.3 | all-reduce | flops 3072 | bytes 12288 | tf_op jit(solution)/shard_map/psum | solution.py:66
  346.8 0.6 multiply_add_fusion
  347.4 109.3 %all-reduce.4.cloned.1.call-done = bf16[3072,256]{1,0:T(8,128)(2,1)} async-done(((bf16[3072,256]{1,0:T(8,128)(2,1)}), bf16[3072,256]{1,0:T(8,128)(2,1)}) %all-reduce.4.cloned.1.call-update) | async-done | bytes 1572880 | tf_op jit(solution)/shard_map/psum | solution.py:65
  456.7 3.0 add_convert_fusion
  (37 shorter events, 0.9 us)
Async XLA Ops:
  7.2 18.0 %copy-start = (bf16[256,2048]{1,0:T(8,128)(2,1)S(1)}, bf16[256,2048]{1,0:T(8,128)(2,1)}, u32[]{:S(2)}) copy-start(bf16[256,2048]{1,0:T(8,128)(2,1)} %param.19) | copy-start | bytes 3145732
  7.2 17.6 %copy-start.4 = (bf16[64,256]{1,0:T(8,128)(2,1)S(1)}, bf16[64,256]{1,0:T(8,128)(2,1)}, u32[]{:S(2)}) copy-start(bf16[64,256]{1,0:T(8,128)(2,1)} %param.18) | copy-start | bytes 98308
  7.2 17.6 %copy-start.5 = (bf16[256,256]{1,0:T(8,128)(2,1)S(1)}, bf16[256,256]{1,0:T(8,128)(2,1)}, u32[]{:S(2)}) copy-start(bf16[256,256]{1,0:T(8,128)(2,1)} %param.21) | copy-start | bytes 393220
  7.2 17.7 %copy-start.3 = (bf16[256,256]{1,0:T(8,128)(2,1)S(1)}, bf16[256,256]{1,0:T(8,128)(2,1)}, u32[]{:S(2)}) copy-start(bf16[256,256]{1,0:T(8,128)(2,1)} %param.20) | copy-start | bytes 393220
  7.2 17.7 %copy-start.8 = (f32[256]{0:T(256)S(1)}, f32[256]{0:T(256)}, u32[]{:S(2)}) copy-start(f32[256]{0:T(256)} %param.22) | copy-start | bytes 3076
  10.1 15.4 %copy-start.10 = (bf16[64,2048]{1,0:T(8,128)(2,1)S(1)}, bf16[64,2048]{1,0:T(8,128)(2,1)}, u32[]{:S(2)}) copy-start(bf16[64,2048]{1,0:T(8,128)(2,1)} %param.23) | copy-start | bytes 786436
  10.1 42.4 %all-to-all-start = ((bf16[64,32,256]{2,0,1:T(8,128)(2,1)}), bf16[64,32,256]{2,0,1:T(8,128)(2,1)}, u32[]{:S(2)}, u32[]{:S(2)}) async-start(bf16[64,32,256]{2,0,1:T(8,128)(2,1)} %copy.21), calls=%async_computation | async-start | bytes 2097152 | tf_op jit(solution)/shard_map/all_to_all | solution.py:26
  24.7 293.6 %all-reduce.6.cloned.1.call-start = ((), (), s32[]{:S(2)}) async-start(), calls=%async_computation.2 | async-start | bytes 5242880
  29.8 2.7 copy-start.2
  37.3 0.8 copy-start.9
  37.3 0.9 copy-start.6
  37.3 1.5 copy-start.1
  37.3 2.0 copy-start.7
  37.3 419.4 %all-reduce.4.cloned.1.call-start = ((), (), s32[]{:S(2)}) async-start(), calls=%async_computation.1 | async-start | bytes 3145728 | tf_op jit(solution)/shard_map/psum | solution.py:65
Sparse Core Ops, SparseCore 0:
  37.5 280.8 all-reduce.5
  321.8 134.8 all-reduce.3
where the time goes:
time: 475 us; the launch traced here: 467 us
  waiting for transfers between devices  383 us (81%)
  blocking collectives  26.8 us (6%)
  between operations  15 us (3%)
  starting transfers between devices  14.7 us (3%)
  local copies, waits for them, and re-layouts  12.7 us (3%)
  matrix products  8.66 us (2%)
  other arithmetic  5.6 us (1%)
    unnamed x3, waiting for transfers between devices  261 us
    psum x1, waiting for transfers between devices, on_device(): lax.psum(own_slab.astype(jnp.bfloat16), 'rep').astype(jnp.float32)  109 us
    psum x1, blocking collectives, on_device(): lax.psum(own_state.astype(jnp.bfloat16), 'rep').astype(jnp.float32)  26.8 us
    all_to_all x1, starting transfers between devices, on_device(): lax.all_to_all(pooled_cot, 'shard', split_axis=1, concat_axis=0, tiled=True)  14.6 us
    all_to_all x1, waiting for transfers between devices, on_device(): lax.all_to_all(pooled_cot, 'shard', split_axis=1, concat_axis=0, tiled=True)  13.1 us
  transfers between devices with their start and end apart: 3, of which 3 were waited for; matrix products, arithmetic and copies ran while one was open for 4% of the time, Pallas kernels for 0%

commit v1 on v0

v1 whole, which is shorter than its diff:
```python
import functools

import jax
import jax.numpy as jnp
from jax import lax
from jax.experimental import pallas as pl
from jax.experimental.pallas import tpu as pltpu
from jax.sharding import PartitionSpec as P

MESH = pl.DeviceIdType.MESH
BLOCK = 128
NS = 32
NR = 16
NY = 8
LEARN = 0.5
BF = jnp.bfloat16
F32 = jnp.float32


def remote(src, dst, send, recv, rep, shard):
    return pltpu.make_async_remote_copy(
        src_ref=src,
        dst_ref=dst,
        send_sem=send,
        recv_sem=recv,
        device_id={"rep": rep, "shard": shard},
        device_id_type=MESH,
    )


def matmul(a, b):
    return jnp.dot(a, b, preferred_element_type=F32)


def matmul_nt(a, b):
    return lax.dot_general(a, b, (((1,), (1,)), ((), ())), preferred_element_type=F32)


def matmul_tn(a, b):
    return lax.dot_general(a, b, (((0,), (0,)), ((), ())), preferred_element_type=F32)


def exchange(
    pooled,
    ids,
    accum,
    listed,
    counts,
    xz,
    w_top,
    u_proj,
    v_proj,
    bias,
    d_act,
    rows_out,
    stats_out,
    blocks_out,
    dense_out,
    wide,
    a_src,
    a_dst,
    hits,
    cols,
    l_dst,
    x_dst,
    part,
    part_dst,
    a_send,
    a_recv,
    l_send,
    l_recv,
    x_send,
    x_recv,
    own_sem,
    c_send,
    c_recv,
    st_send,
    st_recv,
    p_send,
    p_recv,
):
    rep = lax.axis_index("rep")
    shard = lax.axis_index("shard")

    barrier = pltpu.get_barrier_semaphore()

    @pl.loop(1, NS)
    def _(p):
        pl.semaphore_signal(
            barrier, inc=1, device_id={"rep": rep, "shard": lax.rem(shard + p, NS)}, device_id_type=MESH
        )

    @pl.loop(1, NR)
    def _(p):
        pl.semaphore_signal(
            barrier, inc=1, device_id={"rep": lax.rem(rep + p, NR), "shard": shard}, device_id_type=MESH
        )

    samples, feats, width = pooled.shape
    for c in range(0, samples, 16):
        taken = pooled[c : c + 16].astype(F32).reshape(16 * feats, width)
        wide[0, pl.ds(c * feats, 16 * feats), :] = taken[:, :128]
        wide[1, pl.ds(c * feats, 16 * feats), :] = taken[:, 128:]

    pl.semaphore_wait(barrier, NS + NR - 2)

    def pick(h, f):
        return wide[h, pl.ds(f, samples, stride=feats), :].astype(BF)

    def a_out(h, p):
        t = lax.rem(shard + p, NS)
        return remote(a_src.at[h, t], a_dst.at[h, shard], a_send.at[h, p], a_recv.at[h, shard], rep, t)

    def a_in(h, p):
        t = lax.rem(shard + p, NS)
        return remote(a_src.at[h, t], a_dst.at[h, t], a_send.at[h, p], a_recv.at[h, t], rep, t)

    @pl.loop(1, NS)
    def _(p):
        t = lax.rem(shard + p, NS)
        a_src[0, t] = pick(0, t)
        a_out(0, p).start()

    @pl.loop(1, NS)
    def _(p):
        t = lax.rem(shard + p, NS)
        a_src[1, t] = pick(1, t)
        a_out(1, p).start()

    for h in range(2):
        a_dst[h, shard] = pick(h, shard)

    def x_copy(p, slot):
        t = lax.rem(rep + p, NR)
        return remote(xz, x_dst.at[slot(t)], x_send.at[p], x_recv.at[slot(t)], t, shard)

    def l_copy(p, slot):
        t = lax.rem(rep + p, NR)
        at = pl.multiple_of(((5 * t) // 4) * 128, 128)
        return remote(cols.at[:, pl.ds(at, 256)], l_dst.at[slot(t)], l_send.at[p], l_recv.at[slot(t)], t, shard)

    mine, theirs = (lambda t: rep), (lambda t: t)

    @pl.loop(1, NR)
    def _(p):
        x_copy(p, mine).start()

    x = xz[...]
    x_dst[rep] = x
    x_wide = x.astype(F32)
    hid = matmul(x, v_proj[...]).astype(BF)
    mixed = matmul_nt(hid, u_proj[...]) + bias[...]
    x_one = (x_wide * mixed + x_wide).astype(BF)
    hidden = d_act.shape[1]
    back = jnp.zeros((samples, width), F32)
    for c in range(0, hidden, 512):
        z = matmul(x_one, w_top[:, c : c + 512])
        sig = jax.nn.sigmoid(z)
        dz = (d_act[:, c : c + 512].astype(F32) * sig * (1.0 + z * (1.0 - sig))).astype(BF)
        cols[:, c : c + 512] = dz
        back = back + matmul_nt(dz, w_top[:, c : c + 512])
    dp = (back * x_wide).astype(BF)
    cols[:, hidden : hidden + width] = dp
    cols[:, hidden + width : hidden + 2 * width] = dp

    @pl.loop(1, NR)
    def _(p):
        l_copy(p, mine).start()

    own_at = pl.multiple_of(((5 * rep) // 4) * 128, 128)
    own_copy = pltpu.make_async_copy(cols.at[:, pl.ds(own_at, 256)], l_dst.at[rep], own_sem)
    own_copy.start()

    slots = listed.shape[1]
    lookups = ids.shape[1]
    for k in range(slots):
        first = jnp.where(counts[0, 0] > k, listed[0, k] * BLOCK, -(1 << 20))
        for c in range(0, lookups, 512):
            rel = ids[:, c : c + 512] - first
            row = lax.broadcasted_iota(jnp.int32, (BLOCK, 512), 0)
            hit = jnp.zeros((BLOCK, 512), F32)
            for pos in range(ids.shape[0]):
                hit = hit + jnp.where(row == rel[pos : pos + 1, :], 1.0, 0.0)
            hits[k * BLOCK : (k + 1) * BLOCK, c : c + 512] = hit.astype(BF)

    y = rep // 2
    xl = lax.rem(rep, 2)

    def at(dy, flip):
        return lax.rem(y + dy + NY, NY) * 2 + ((1 - xl) if flip else xl)

    up, down, across = at(1, False), at(-1, False), at(0, True)
    started = []
    counter = [0]

    def ref_of(h, q, half):
        if half is None:
            return rows_out.at[h, q]
        return rows_out.at[h, q, pl.ds(half * BLOCK, BLOCK)]

    def c_start(h, q, to, half=None):
        copy = remote(
            ref_of(h, q, half), ref_of(h, q, half), c_send.at[counter[0]], c_recv.at[h, q, half or 0], to, shard
        )
        counter[0] += 1
        copy.start()
        started.append(copy)

    def c_wait(h, q, half=None):
        remote(ref_of(h, q, half), ref_of(h, q, half), c_send.at[0], c_recv.at[h, q, half or 0], across, shard).wait_recv()

    def step1(h):
        for to in (up, down, across):
            c_start(h, rep, to)

    def step2(h):
        for dy, to in ((-1, up), (1, down)):
            c_wait(h, at(dy, False))
            c_start(h, at(dy, False), to)
        c_wait(h, across)
        for to in (up, down):
            c_start(h, across, to)

    def step3(h):
        for dy, to in ((-1, up), (1, down)):
            c_wait(h, at(2 * dy, False))
            c_start(h, at(2 * dy, False), to)
        for dy, to in ((-1, up), (1, down)):
            c_wait(h, at(dy, True))
            c_start(h, at(dy, True), to)

    def step4(h):
        for dy, to, half in ((-1, up, 0), (1, down, 1)):
            c_wait(h, at(3 * dy, False))
            c_start(h, at(3 * dy, False), to, half)
            c_start(h, at(3 * dy, False), across)

    def step5(h):
        for half in (0, 1):
            c_wait(h, at(4, False), half)
            c_start(h, at(4, False), across, half)

    def step6(h):
        for dy in (-2, 2, -3, 3):
            c_wait(h, at(dy, True))
        for half in (0, 1):
            c_wait(h, at(4, True), half)

    def gradient(h):
        @pl.loop(1, NS)
        def _(p):
            a_in(h, p).wait_recv()

        grad = matmul(hits[...], a_dst[h].reshape(lookups, 128))
        rows_out[h, rep] = grad.astype(BF)
        step1(h)
        return jnp.sum(grad * grad, axis=1, keepdims=True)

    square = gradient(0)
    step2(0)
    step3(0)
    square = (square + gradient(1)) * (1.0 / width)

    diag = lax.broadcasted_iota(jnp.int32, (BLOCK, BLOCK), 0) == lax.broadcasted_iota(jnp.int32, (BLOCK, BLOCK), 1)
    change, scale, block = [], [], []
    for k in range(slots):
        col = jnp.broadcast_to(square[k * BLOCK : (k + 1) * BLOCK], (BLOCK, BLOCK))
        mean = jnp.sum(jnp.where(diag, col, 0.0), axis=0, keepdims=True)
        old = accum[pl.ds(listed[0, k], 1), :]
        change.append(mean)
        scale.append(LEARN * lax.rsqrt(old + mean))
        block.append(jnp.full((1, BLOCK), listed[0, k].astype(F32), F32))
    stats_out[rep] = jnp.concatenate(change + scale + block + [jnp.zeros((2, BLOCK), F32)], axis=0)

    def st_copy(p, slot):
        t = lax.rem(rep + p, NR)
        return remote(stats_out.at[slot(t)], stats_out.at[slot(t)], st_send.at[p], st_recv.at[slot(t)], t, shard)

    @pl.loop(1, NR)
    def _(p):
        st_copy(p, mine).start()

    step4(0)
    step2(1)
    step5(0)
    step3(1)
    step4(1)

    @pl.loop(1, NR)
    def _(p):
        x_copy(p, theirs).wait_recv()
        l_copy(p, theirs).wait_recv()

    own_copy.wait()
    many = NR * samples
    xs = x_dst[...].reshape(many, width)
    ls = l_dst[...].reshape(many, width)
    xs_wide = xs.astype(F32)
    hids = matmul(xs, v_proj[...]).astype(BF)
    ones = (xs_wide * (matmul_nt(hids, u_proj[...]) + bias[...]) + xs_wide).astype(BF)
    low, high = u_proj[: width // 2, :], u_proj[width // 2 :, :]
    swapped = rep == 14
    dhs = (
        matmul(ls[:, : width // 2], jnp.where(swapped, high, low))
        + matmul(ls[:, width // 2 :], jnp.where(swapped, low, high))
    ).astype(BF)
    source = lax.broadcasted_iota(jnp.int32, (width, width), 0)
    target = lax.broadcasted_iota(jnp.int32, (width, width), 1)
    wanted = (target // 8) * 5 + target % 8

    def spread(values, offset):
        chosen = (source == wanted + offset) & (target % 8 < 5)
        return matmul(values, jnp.where(chosen, 1.0, 0.0).astype(BF)).astype(BF)

    left_a = spread(ls, 32 * lax.rem(rep, 4))
    total_a = matmul_tn(left_a, jnp.where(rep <= 12, ones, hids))
    offset_b = jnp.where(rep == 12, 0, jnp.where(rep == 14, -64, 96))
    left_b = spread(jnp.where(rep <= 12, ls, xs), offset_b)
    total_b = matmul_tn(left_b, jnp.where(rep <= 12, hids, dhs))
    limit = jnp.where(rep == 12, 128, jnp.where(rep == 14, 64, jnp.where(rep == 15, 0, 160)))
    line = lax.broadcasted_iota(jnp.int32, (width, width), 0)
    grow = jnp.where((line // 8) * 5 + line % 8 < limit, total_a, total_b)
    part[...] = grow.reshape(NS, 8, width)
    part_dst[shard] = part[shard]

    def p_copy(p, slot):
        t = lax.rem(shard + p, NS)
        return remote(part.at[t], part_dst.at[slot(t)], p_send.at[p], p_recv.at[slot(t)], rep, t)

    own_shard, that_shard = (lambda t: shard), (lambda t: t)

    @pl.loop(1, NS)
    def _(p):
        p_copy(p, own_shard).start()

    step5(1)
    step6(0)
    step6(1)

    @pl.loop(1, NR)
    def _(p):
        st_copy(p, theirs).wait_recv()

    lane = lax.broadcasted_iota(jnp.int32, (1, BLOCK), 1)
    blocks = jnp.zeros((1, BLOCK), F32)
    for r in range(NR):
        for k in range(slots):
            row = stats_out[r, 2 * slots + k : 2 * slots + k + 1, :]
            blocks = blocks + jnp.where(lane == r * slots + k, row, 0.0)
    blocks_out[...] = blocks.astype(jnp.int32)

    @pl.loop(1, NS)
    def _(p):
        p_copy(p, that_shard).wait_recv()

    dense_out[...] = jnp.sum(part_dst[...], axis=0)

    @pl.loop(1, NS)
    def _(p):
        a_out(0, p).wait_send()
        a_out(1, p).wait_send()
        p_copy(p, own_shard).wait_send()

    @pl.loop(1, NR)
    def _(p):
        x_copy(p, mine).wait_send()
        l_copy(p, mine).wait_send()
        st_copy(p, mine).wait_send()

    for copy in started:
        copy.wait_send()


def apply(norm, blocks, table, accum, rows, stats, dense, table_out, accum_out, dense_out, total, state):
    nblk, block, width = table.shape
    reps = rows.shape[1]
    slots = 2
    total[...] = jnp.zeros_like(total)
    state[...] = jnp.zeros_like(state)
    for r in range(reps):
        scales = jnp.transpose(jnp.concatenate([stats[r, :, :]] * 16, axis=0))
        for k in range(slots):
            b = blocks[0, r * slots + k]
            col = scales[:, slots + k : slots + k + 1]
            for h in range(2):
                g = rows[h, r, k * block : (k + 1) * block, :].astype(F32)
                total[b, :, h * 128 : (h + 1) * 128] += g * col
            state[pl.ds(b, 1), :] += stats[r, k : k + 1, :]
    for b in range(nblk):
        table_out[b] = (table[b].astype(F32) - total[b] * (1.0 / reps)).astype(BF)
    accum_out[...] = accum[...] + state[...] * (1.0 / reps)
    for j in range(5):
        for h in range(2):
            dense_out[2 * j + h : 2 * j + h + 1, :] = dense[j : j + 1, h * 128 : (h + 1) * 128] * norm


def on_device(
    pooled_cot,
    bag_ids,
    table,
    accum,
    listed_block_index,
    counts,
    x_zero,
    w_top,
    u_proj,
    v_proj,
    cross_bias,
    d_act,
):
    width = table.shape[1]
    nblk = table.shape[0] // BLOCK
    samples, feats = pooled_cot.shape[:2]
    hidden = d_act.shape[1]
    slots = listed_block_index.shape[1]
    listed_rows = slots * BLOCK
    lookups = bag_ids.shape[0]
    vmem = pl.BlockSpec(memory_space=pltpu.VMEM)
    smem = pl.BlockSpec(memory_space=pltpu.SMEM)
    dma = pltpu.SemaphoreType.DMA
    ids = jnp.transpose(bag_ids.reshape(lookups, bag_ids.shape[2]))
    state = accum.reshape(nblk, BLOCK)
    rows, stats, blocks, dense = pl.pallas_call(
        exchange,
        out_shape=(
            jax.ShapeDtypeStruct((2, NR, listed_rows, 128), BF),
            jax.ShapeDtypeStruct((NR, 8, BLOCK), F32),
            jax.ShapeDtypeStruct((1, BLOCK), jnp.int32),
            jax.ShapeDtypeStruct((8, width), F32),
        ),
        in_specs=[vmem, vmem, vmem, smem, smem, vmem, vmem, vmem, vmem, vmem, vmem],
        out_specs=(vmem, vmem, vmem, vmem),
        scratch_shapes=[
            pltpu.VMEM((2, samples * feats, 128), F32),
            pltpu.VMEM((2, NS, samples, 128), BF),
            pltpu.VMEM((2, NS, samples, 128), BF),
            pltpu.VMEM((listed_rows, lookups), BF),
            pltpu.VMEM((samples, hidden + 2 * width), BF),
            pltpu.VMEM((NR, samples, width), BF),
            pltpu.VMEM((NR, samples, width), BF),
            pltpu.VMEM((NS, 8, width), F32),
            pltpu.VMEM((NS, 8, width), F32),
            dma((2, NS)),
            dma((2, NS)),
            dma((NR,)),
            dma((NR,)),
            dma((NR,)),
            dma((NR,)),
            dma,
            dma((64,)),
            dma((2, NR, 2)),
            dma((NR,)),
            dma((NR,)),
            dma((NS,)),
            dma((NS,)),
        ],
        compiler_params=pltpu.CompilerParams(
            collective_id=0, has_side_effects=True, vmem_limit_bytes=40 << 20
        ),
        name="exchange",
    )(
        pooled_cot,
        ids,
        state,
        listed_block_index,
        counts,
        x_zero,
        w_top,
        u_proj,
        v_proj,
        cross_bias.reshape(1, width),
        d_act,
    )
    total = samples * lax.axis_size("rep") * lax.axis_size("shard")
    new_table, new_accum, out = pl.pallas_call(
        functools.partial(apply, float(total) ** -0.5),
        out_shape=(
            jax.ShapeDtypeStruct((nblk, BLOCK, width), BF),
            jax.ShapeDtypeStruct((nblk, BLOCK), F32),
            jax.ShapeDtypeStruct((10, 128), F32),
        ),
        in_specs=[smem, vmem, vmem, vmem, vmem, vmem],
        out_specs=(vmem, vmem, vmem),
        scratch_shapes=[pltpu.VMEM((nblk, BLOCK, width), F32), pltpu.VMEM((nblk, BLOCK), F32)],
        compiler_params=pltpu.CompilerParams(vmem_limit_bytes=24 << 20),
        name="apply",
    )(blocks, table.reshape(nblk, BLOCK, width), state, rows, stats, dense)
    return (new_table.reshape(table.shape), new_accum.reshape(accum.shape), out.reshape(1280))


def solution(mesh):
    return jax.shard_map(
        on_device,
        mesh=mesh,
        in_specs=(
            P(("rep", "shard"), None, None),
            P("rep", "shard", None),
            P("shard", None),
            P("shard"),
            P("rep", "shard"),
            P("rep", "shard"),
            P(("rep", "shard"), None),
            P(),
            P(),
            P(),
            P(),
            P(("rep", "shard"), None),
        ),
        out_specs=(P("shard", None), P("shard"), P(("rep", "shard"))),
        check_vma=False,
    )
```

time: 475 us -> 90.4 us (0.19); the launches traced: 467 us -> 90 us
  waiting for transfers between devices: 383 us -> 0 us
  Pallas kernels: 0 us -> 79.8 us
  blocking collectives: 26.8 us -> 0 us
  starting transfers between devices: 14.7 us -> 0 us
  between operations: 15 us -> 1.44 us
  matrix products: 8.66 us -> 0 us
  other arithmetic: 5.6 us -> 0 us
    unnamed x3 -> x0, waiting for transfers between devices: 261 us -> none
    psum x1 -> x0, waiting for transfers between devices: 109 us -> none  [on_device(): lax.psum(own_slab.astype(jnp.bfloat16), 'rep').astype(jnp.float32)]
    pallas_call x0 -> x2, Pallas kernels: none -> 79.8 us  [the longest x1 76.3 us: on_device(): pl.pallas_call(exchange, out_shape=(jax.ShapeDtypeStruct((2, NR, listed_r...]
    psum x1 -> x0, blocking collectives: 26.8 us -> none  [on_device(): lax.psum(own_state.astype(jnp.bfloat16), 'rep').astype(jnp.float32)]
    all_to_all x1 -> x0, starting transfers between devices: 14.6 us -> none  [on_device(): lax.all_to_all(pooled_cot, 'shard', split_axis=1, concat_axis=0, tiled=True)]
    all_to_all x1 -> x0, waiting for transfers between devices: 13.1 us -> none  [on_device(): lax.all_to_all(pooled_cot, 'shard', split_axis=1, concat_axis=0, tiled=True)]
    dot_general x10 -> x0, matrix products: 8.66 us -> none  [the longest x1 1.88 us: on_device(): jnp.dot(lookup_hits, pooled_rows, preferred_element_type=jnp.float32)]
  transfers between devices with their start and end apart: 3 -> 0, of which waited for: 3 -> 0; matrix products, arithmetic and copies ran while one was open for 4% -> 0% of each run, Pallas kernels for 0% -> 0%
where the time goes in v1:
time: 90.4 us; the launch traced here: 90 us
  Pallas kernels  79.8 us (88%)
  local copies, waits for them, and re-layouts  8.72 us (10%)
  between operations  1.44 us (2%)
    pallas_call x1, Pallas kernels, on_device(): pl.pallas_call(exchange, out_shape=(jax.ShapeDtypeStruct((2, NR, listed_r...  76.3 us
    unnamed x22, local copies, waits for them, and re-layouts  8.72 us
    pallas_call x1, Pallas kernels, on_device(): pl.pallas_call(functools.partial(apply, float(total) ** (-0.5)), out_shap...  3.54 us

profile of v1, /device:TPU:1, one launch (start us, length us, event | category | flops | bytes accessed | tf_op | source)
XLA Modules:
  0.0 90.0 jit_solution(14961033087624612672)
XLA Ops:
  0.6 0.0 copy-start
  1.4 0.0 copy-start.1
  1.4 1.2 %copy-done.1 = bf16[64,32,256]{2,1,0:T(8,128)(2,1)S(1)} copy-done((bf16[64,32,256]{2,1,0:T(8,128)(2,1)S(1)}, bf16[64,32,256]{2,1,0:T(8,128)(2,1)}, u32[]{:S(2)}) %copy-start.1) | copy-done | bytes 1048600
  2.6 0.0 copy-start.2
  2.6 1.2 %copy-done.2 = bf16[256,2048]{1,0:T(8,128)(2,1)S(1)} copy-done((bf16[256,2048]{1,0:T(8,128)(2,1)S(1)}, bf16[256,2048]{1,0:T(8,128)(2,1)}, u32[]{:S(2)}) %copy-start.2) | copy-done | bytes 1048600
  3.9 0.0 copy-start.3
  3.9 0.9 %copy-done.3 = bf16[64,2048]{1,0:T(8,128)(2,1)S(1)} copy-done((bf16[64,2048]{1,0:T(8,128)(2,1)S(1)}, bf16[64,2048]{1,0:T(8,128)(2,1)}, u32[]{:S(2)}) %copy-start.3) | copy-done | bytes 262168
  4.8 0.0 copy-start.4
  4.8 0.9 %copy-done.4 = bf16[256,256]{1,0:T(8,128)(2,1)S(1)} copy-done((bf16[256,256]{1,0:T(8,128)(2,1)S(1)}, bf16[256,256]{1,0:T(8,128)(2,1)}, u32[]{:S(2)}) %copy-start.4) | copy-done | bytes 131096
  5.7 0.0 copy-start.5
  5.7 0.9 %copy-done.5 = bf16[256,256]{1,0:T(8,128)(2,1)S(1)} copy-done((bf16[256,256]{1,0:T(8,128)(2,1)S(1)}, bf16[256,256]{1,0:T(8,128)(2,1)}, u32[]{:S(2)}) %copy-start.5) | copy-done | bytes 131096
  6.6 0.0 copy-start.6
  6.6 0.7 copy-done.6
  7.3 0.0 copy-start.7
  7.3 0.8 copy-done.7
  8.1 0.0 copy-start.8
  8.1 0.7 copy-done.8
  8.8 0.0 copy-start.9
  8.8 0.7 copy-done.9
  9.5 0.0 copy-start.10
  9.5 0.7 copy-done.10
  10.1 76.3 %exchange.1 = (bf16[2,16,256,128]{3,2,1,0:T(8,128)(2,1)S(1)}, f32[16,8,128]{2,1,0:T(8,128)S(1)}, s32[1,128]{1,0:T(1,128)S(1)}, f32[8,256]{1,0:T(8,128)S(1)}) custom-call(bf16[64,32,256]{2,1,0:T(8,128)(2,1)S(1)} %copy-done.1, s32[2,2048]{1,0:T(2,128)S(1)} %bitcast.12, f32[24,128]{1,0:T(8,128)S(1)} %bitcast.10, s32[1,2]{1,0:T(1,128)S(1)} %copy-done.10, ...), custom_call_target="tpu_custom_call" | custom-call | tf_op jit(solution)/shard_map/exchange/pallas_call | solution.py:423
  86.4 0.0 copy-done
  86.4 3.5 %apply.1 = (bf16[24,128,256]{2,1,0:T(8,128)(2,1)}, f32[24,128]{1,0:T(8,128)}, f32[10,128]{1,0:T(8,128)}) custom-call(s32[1,128]{1,0:T(1,128)S(1)} %get-tuple-element.10.blocks, bf16[24,128,256]{2,1,0:T(8,128)(2,1)S(1)} %bitcast.9, f32[24,128]{1,0:T(8,128)S(1)} %bitcast.11, bf16[2,16,256,128]{3,2,1,0:T(8,128)(2,1)S(1)} %get-tuple-element.11.rows, ...), custom_call_target="tpu_custom_call" | custom-call | tf_op jit(solution)/shard_map/apply/pallas_call | solution.py:475
Async XLA Ops:
  0.6 85.8 %copy-start = (bf16[3072,256]{1,0:T(8,128)(2,1)S(1)}, bf16[3072,256]{1,0:T(8,128)(2,1)}, u32[]{:S(2)}) copy-start(bf16[3072,256]{1,0:T(8,128)(2,1)} %param.14) | copy-start | bytes 4718596
  1.4 1.2 %copy-start.1 = (bf16[64,32,256]{2,1,0:T(8,128)(2,1)S(1)}, bf16[64,32,256]{2,1,0:T(8,128)(2,1)}, u32[]{:S(2)}) copy-start(bf16[64,32,256]{2,1,0:T(8,128)(2,1)} %pooled.1) | copy-start | bytes 3145732
  2.6 1.2 %copy-start.2 = (bf16[256,2048]{1,0:T(8,128)(2,1)S(1)}, bf16[256,2048]{1,0:T(8,128)(2,1)}, u32[]{:S(2)}) copy-start(bf16[256,2048]{1,0:T(8,128)(2,1)} %w_top.1) | copy-start | bytes 3145732
  3.9 0.9 %copy-start.3 = (bf16[64,2048]{1,0:T(8,128)(2,1)S(1)}, bf16[64,2048]{1,0:T(8,128)(2,1)}, u32[]{:S(2)}) copy-start(bf16[64,2048]{1,0:T(8,128)(2,1)} %d_act.1) | copy-start | bytes 786436
  4.8 0.9 %copy-start.4 = (bf16[256,256]{1,0:T(8,128)(2,1)S(1)}, bf16[256,256]{1,0:T(8,128)(2,1)}, u32[]{:S(2)}) copy-start(bf16[256,256]{1,0:T(8,128)(2,1)} %u_proj.1) | copy-start | bytes 393220
  5.7 0.9 %copy-start.5 = (bf16[256,256]{1,0:T(8,128)(2,1)S(1)}, bf16[256,256]{1,0:T(8,128)(2,1)}, u32[]{:S(2)}) copy-start(bf16[256,256]{1,0:T(8,128)(2,1)} %v_proj.1) | copy-start | bytes 393220
  6.6 0.7 copy-start.6
  7.3 0.8 copy-start.7
  8.1 0.7 copy-start.8
  8.8 0.7 copy-start.9
  9.5 0.7 copy-start.10

commit v2 on v1

v2 whole, which is shorter than its diff:
```python
import functools

import jax
import jax.numpy as jnp
from jax import lax
from jax.experimental import pallas as pl
from jax.experimental.pallas import tpu as pltpu
from jax.sharding import PartitionSpec as P

MESH = pl.DeviceIdType.MESH
BLOCK = 128
NS = 32
NR = 16
NY = 8
LEARN = 0.5
BF = jnp.bfloat16
F32 = jnp.float32


def remote(src, dst, send, recv, rep, shard):
    return pltpu.make_async_remote_copy(
        src_ref=src,
        dst_ref=dst,
        send_sem=send,
        recv_sem=recv,
        device_id={"rep": rep, "shard": shard},
        device_id_type=MESH,
    )


def matmul(a, b):
    return jnp.dot(a, b, preferred_element_type=F32)


def matmul_nt(a, b):
    return lax.dot_general(a, b, (((1,), (1,)), ((), ())), preferred_element_type=F32)


def matmul_tn(a, b):
    return lax.dot_general(a, b, (((0,), (0,)), ((), ())), preferred_element_type=F32)


def exchange(
    pooled_in,
    ids_in,
    accum_in,
    listed_in,
    counts_in,
    xz_in,
    w_top_in,
    u_proj_in,
    v_proj_in,
    bias_in,
    d_act_in,
    rows_hbm,
    stats_hbm,
    blocks_hbm,
    dense_hbm,
    rows_out,
    stats_out,
    blocks_out,
    dense_out,
    out_sem,
    pooled,
    ids,
    accum,
    listed,
    counts,
    xz,
    w_top,
    u_proj,
    v_proj,
    bias,
    d_act,
    in_sem,
    wide,
    a_src,
    a_dst,
    hits,
    hid_all,
    right,
    cols,
    l_dst,
    x_dst,
    part,
    part_dst,
    a_send,
    a_recv,
    l_send,
    l_recv,
    x_send,
    x_recv,
    own_sem,
    c_send,
    c_recv,
    st_send,
    st_recv,
    p_send,
    p_recv,
):
    rep = lax.axis_index("rep")
    shard = lax.axis_index("shard")

    samples, feats, width = pooled.shape
    chunk = samples // 4
    pairs = tuple((pooled_in.at[pl.ds(i * chunk, chunk)], pooled.at[pl.ds(i * chunk, chunk)]) for i in range(4)) + (
        (xz_in, xz),
        (v_proj_in, v_proj),
        (u_proj_in, u_proj),
        (bias_in, bias),
        (w_top_in, w_top),
        (d_act_in, d_act),
        (listed_in, listed),
        (counts_in, counts),
        (ids_in, ids),
        (accum_in, accum),
    )
    fetched = [pltpu.make_async_copy(src, dst, in_sem.at[i]) for i, (src, dst) in enumerate(pairs)]
    for copy in fetched:
        copy.start()

    barrier = pltpu.get_barrier_semaphore()

    @pl.loop(1, NS)
    def _(p):
        pl.semaphore_signal(
            barrier, inc=1, device_id={"rep": rep, "shard": lax.rem(shard + p, NS)}, device_id_type=MESH
        )

    @pl.loop(1, NR)
    def _(p):
        pl.semaphore_signal(
            barrier, inc=1, device_id={"rep": lax.rem(rep + p, NR), "shard": shard}, device_id_type=MESH
        )

    for i in range(4):
        fetched[i].wait()
        taken = pooled[i * chunk : (i + 1) * chunk].astype(F32).reshape(chunk * feats, width)
        wide[0, pl.ds(i * chunk * feats, chunk * feats), :] = taken[:, :128]
        wide[1, pl.ds(i * chunk * feats, chunk * feats), :] = taken[:, 128:]

    pl.semaphore_wait(barrier, NS + NR - 2)

    stored = []

    def store(src, dst):
        copy = pltpu.make_async_copy(src, dst, out_sem.at[len(stored)])
        copy.start()
        stored.append(copy)

    y = rep // 2
    xl = lax.rem(rep, 2)

    def at(dy, flip):
        return lax.rem(y + dy + NY, NY) * 2 + ((1 - xl) if flip else xl)

    across = at(0, True)

    class Gather:
        def __init__(self, ref, send, recv, diagonal, out=None):
            self.ref, self.send, self.recv, self.diagonal, self.out = ref, send, recv, diagonal, out
            self.copies = []

        def view(self, ref, q, half):
            if half is None:
                return ref.at[q]
            rows = ref.shape[1] // 2
            return ref.at[q, pl.ds(half * rows, rows)]

        def start(self, q, to, half=None):
            ref = self.view(self.ref, q, half)
            copy = remote(ref, ref, self.send.at[len(self.copies)], self.recv.at[q, half or 0], to, shard)
            copy.start()
            self.copies.append(copy)

        def wait(self, q, half=None):
            ref = self.view(self.ref, q, half)
            remote(ref, ref, self.send.at[0], self.recv.at[q, half or 0], across, shard).wait_recv()
            if self.out is not None:
                store(ref, self.view(self.out, q, half))

        def begin(self):
            for to in (at(2, False), at(-2, False), at(1, False), at(-1, False), across):
                self.start(rep, to)

        def middle(self):
            for side, half in ((1, 0), (-1, 1)):
                q = at(-2 * side, False)
                self.wait(q)
                self.start(q, at(2 * side, False), half)
                self.start(q, at(side, False))
                if self.diagonal:
                    self.start(q, at(side, True))
                self.start(q, across)
            self.wait(across)
            for side in (1, -1):
                self.start(across, at(side, False))

        def late(self):
            for dy in (-3, 3):
                self.wait(at(dy, False))
                if not self.diagonal:
                    self.start(at(dy, False), across)
            for half in (0, 1):
                self.wait(at(4, False), half)
                self.start(at(4, False), across, half)

        def end(self):
            for dy in (-1, 1):
                self.wait(at(dy, False))
            for dy in (-1, 1, -2, 2, -3, 3):
                self.wait(at(dy, True))
            for half in (0, 1):
                self.wait(at(4, True), half)

        def drain(self):
            for copy in self.copies:
                copy.wait_send()

    x_gather = Gather(x_dst, x_send, x_recv, True)
    row_gathers = (
        Gather(rows_out.at[0], c_send.at[0], c_recv.at[0], False),
        Gather(rows_out.at[1], c_send.at[1], c_recv.at[1], True, rows_hbm.at[1]),
    )

    def pick(h, f):
        return wide[h, pl.ds(f, samples, stride=feats), :].astype(BF)

    def a_out(h, p):
        t = lax.rem(shard + p, NS)
        return remote(a_src.at[h, t], a_dst.at[h, shard], a_send.at[h, p], a_recv.at[h, shard], rep, t)

    def a_in(h, p):
        t = lax.rem(shard + p, NS)
        return remote(a_src.at[h, t], a_dst.at[h, t], a_send.at[h, p], a_recv.at[h, t], rep, t)

    @pl.loop(1, NS)
    def _(p):
        t = lax.rem(shard + p, NS)
        a_src[0, t] = pick(0, t)
        a_out(0, p).start()

    def l_copy(p, slot):
        t = lax.rem(rep + p, NR)
        at = pl.multiple_of(((5 * t) // 4) * 128, 128)
        return remote(cols.at[:, pl.ds(at, 256)], l_dst.at[slot(t)], l_send.at[p], l_recv.at[slot(t)], t, shard)

    mine, theirs = (lambda t: rep), (lambda t: t)

    fetched[4].wait()
    x = xz[...]
    x_dst[rep] = x
    x_gather.begin()
    for copy in fetched[5:]:
        copy.wait()
    x_wide = x.astype(F32)
    hid = matmul(x, v_proj[...]).astype(BF)
    mixed = matmul_nt(hid, u_proj[...]) + bias[...]
    x_one = (x_wide * mixed + x_wide).astype(BF)
    hidden = d_act.shape[1]
    back = jnp.zeros((samples, width), F32)
    for c in range(0, hidden, 512):
        z = matmul(x_one, w_top[:, c : c + 512])
        sig = jax.nn.sigmoid(z)
        dz = (d_act[:, c : c + 512].astype(F32) * sig * (1.0 + z * (1.0 - sig))).astype(BF)
        cols[:, c : c + 512] = dz
        back = back + matmul_nt(dz, w_top[:, c : c + 512])
    dp = (back * x_wide).astype(BF)
    cols[:, hidden : hidden + width] = dp
    cols[:, hidden + width : hidden + 2 * width] = dp

    @pl.loop(1, NR)
    def _(p):
        l_copy(p, mine).start()

    own_at = pl.multiple_of(((5 * rep) // 4) * 128, 128)
    own_copy = pltpu.make_async_copy(cols.at[:, pl.ds(own_at, 256)], l_dst.at[rep], own_sem)
    own_copy.start()

    @pl.loop(1, NS)
    def _(p):
        t = lax.rem(shard + p, NS)
        a_src[1, t] = pick(1, t)
        a_out(1, p).start()

    for h in range(2):
        a_dst[h, shard] = pick(h, shard)

    x_gather.middle()

    slots = listed.shape[1]
    lookups = ids.shape[1]
    for k in range(slots):
        first = jnp.where(counts[0, 0] > k, listed[0, k] * BLOCK, -(1 << 20))
        for c in range(0, lookups, 512):
            rel = ids[:, c : c + 512] - first
            row = lax.broadcasted_iota(jnp.int32, (BLOCK, 512), 0)
            hit = jnp.zeros((BLOCK, 512), F32)
            for pos in range(ids.shape[0]):
                hit = hit + jnp.where(row == rel[pos : pos + 1, :], 1.0, 0.0)
            hits[k * BLOCK : (k + 1) * BLOCK, c : c + 512] = hit.astype(BF)

    def gradient(h):
        @pl.loop(1, NS)
        def _(p):
            a_in(h, p).wait_recv()

        grad = matmul(hits[...], a_dst[h].reshape(lookups, 128))
        rows_out[h, rep] = grad.astype(BF)
        row_gathers[h].begin()
        if h == 1:
            store(rows_out.at[h, rep], rows_hbm.at[h, rep])
        return jnp.sum(grad * grad, axis=1, keepdims=True)

    square = gradient(0)
    x_gather.late()
    row_gathers[0].middle()
    square = (square + gradient(1)) * (1.0 / width)

    diag = lax.broadcasted_iota(jnp.int32, (BLOCK, BLOCK), 0) == lax.broadcasted_iota(jnp.int32, (BLOCK, BLOCK), 1)
    change, scale, block = [], [], []
    for k in range(slots):
        col = jnp.broadcast_to(square[k * BLOCK : (k + 1) * BLOCK], (BLOCK, BLOCK))
        mean = jnp.sum(jnp.where(diag, col, 0.0), axis=0, keepdims=True)
        old = accum[pl.ds(listed[0, k], 1), :]
        change.append(mean)
        scale.append(LEARN * lax.rsqrt(old + mean))
        block.append(jnp.full((1, BLOCK), listed[0, k].astype(F32), F32))
    stats_out[rep] = jnp.concatenate(change + scale + block + [jnp.zeros((2, BLOCK), F32)], axis=0)

    def st_copy(p, slot):
        t = lax.rem(rep + p, NR)
        return remote(stats_out.at[slot(t)], stats_out.at[slot(t)], st_send.at[p], st_recv.at[slot(t)], t, shard)

    @pl.loop(1, NR)
    def _(p):
        st_copy(p, mine).start()

    row_gathers[0].late()
    x_gather.end()
    many = NR * samples
    xs = x_dst[...].reshape(many, width)
    hids = matmul(xs, v_proj[...]).astype(BF)
    hid_all[...] = hids

    @pl.when(rep <= 12)
    def _():
        wide_xs = x_dst[...].reshape(many, width).astype(F32)
        mixing = matmul_nt(hid_all[...], u_proj[...]) + bias[...]
        right[...] = (wide_xs * mixing + wide_xs).astype(BF)

    @pl.when(rep > 12)
    def _():
        right[...] = hid_all[...]

    row_gathers[1].middle()

    @pl.loop(1, NR)
    def _(p):
        l_copy(p, theirs).wait_recv()

    own_copy.wait()

    def spread(values, offset):
        source = lax.broadcasted_iota(jnp.int32, (width, width), 0)
        target = lax.broadcasted_iota(jnp.int32, (width, width), 1)
        chosen = (source == (target // 8) * 5 + target % 8 + offset) & (target % 8 < 5)
        return matmul(values, jnp.where(chosen, 1.0, 0.0).astype(BF)).astype(BF)

    line = lax.broadcasted_iota(jnp.int32, (width, width), 0)
    line = (line // 8) * 5 + line % 8

    @pl.when(rep < 15)
    def _():
        left = spread(l_dst[...].reshape(many, width), 32 * lax.rem(rep, 4))
        part[...] = matmul_tn(left, right[...]).reshape(NS, 8, width)

    @pl.when(rep == 12)
    def _():
        left = spread(l_dst[...].reshape(many, width), 0)
        below = matmul_tn(left, hid_all[...])
        part[...] = jnp.where(line < 128, part[...].reshape(width, width), below).reshape(NS, 8, width)

    @pl.when(rep >= 14)
    def _():
        ls = l_dst[...].reshape(many, width)
        low, high = u_proj[: width // 2, :], u_proj[width // 2 :, :]
        dhs = (
            matmul(ls[:, : width // 2], jnp.where(rep == 14, high, low))
            + matmul(ls[:, width // 2 :], jnp.where(rep == 14, low, high))
        ).astype(BF)
        left = spread(x_dst[...].reshape(many, width), jnp.where(rep == 14, -64, 96))
        below = matmul_tn(left, dhs)
        above = jnp.where(rep == 14, part[...].reshape(width, width), below)
        part[...] = jnp.where(line < 64, above, below).reshape(NS, 8, width)

    part_dst[shard] = part[shard]

    def p_copy(p, slot):
        t = lax.rem(shard + p, NS)
        return remote(part.at[t], part_dst.at[slot(t)], p_send.at[p], p_recv.at[slot(t)], rep, t)

    own_shard, that_shard = (lambda t: shard), (lambda t: t)

    @pl.loop(1, NS)
    def _(p):
        p_copy(p, own_shard).start()

    row_gathers[1].late()
    row_gathers[0].end()
    store(rows_out.at[0], rows_hbm.at[0])

    @pl.loop(1, NR)
    def _(p):
        st_copy(p, theirs).wait_recv()

    lane = lax.broadcasted_iota(jnp.int32, (1, BLOCK), 1)
    blocks = jnp.zeros((1, BLOCK), F32)
    for r in range(NR):
        for k in range(slots):
            row = stats_out[r, 2 * slots + k : 2 * slots + k + 1, :]
            blocks = blocks + jnp.where(lane == r * slots + k, row, 0.0)
    blocks_out[...] = blocks.astype(jnp.int32)
    store(stats_out, stats_hbm)
    store(blocks_out, blocks_hbm)
    row_gathers[1].end()

    @pl.loop(1, NS)
    def _(p):
        p_copy(p, that_shard).wait_recv()

    dense_out[...] = jnp.sum(part_dst[...], axis=0)
    store(dense_out, dense_hbm)

    @pl.loop(1, NS)
    def _(p):
        a_out(0, p).wait_send()
        a_out(1, p).wait_send()
        p_copy(p, own_shard).wait_send()

    @pl.loop(1, NR)
    def _(p):
        l_copy(p, mine).wait_send()
        st_copy(p, mine).wait_send()

    x_gather.drain()
    for gather in row_gathers:
        gather.drain()
    for copy in stored:
        copy.wait()


def apply(
    norm,
    blocks_in,
    table_in,
    accum_in,
    rows_in,
    stats_in,
    dense_in,
    table_out,
    accum_out,
    dense_out,
    blocks,
    table,
    accum,
    rows,
    stats,
    dense,
    done,
    total,
    state,
    sems,
    in_sems,
):
    nblk, block, width = table.shape
    reps = rows.shape[1]
    slots = 2
    groups = 4
    per = reps // groups
    pairs = [(blocks_in, blocks), (stats_in, stats)]
    pairs += [(rows_in.at[:, pl.ds(i * per, per)], rows.at[:, pl.ds(i * per, per)]) for i in range(groups)]
    pairs += [(table_in, table), (accum_in, accum), (dense_in, dense)]
    fetched = [pltpu.make_async_copy(src, dst, in_sems.at[i]) for i, (src, dst) in enumerate(pairs)]
    for copy in fetched:
        copy.start()
    total[...] = jnp.zeros_like(total)
    state[...] = jnp.zeros_like(state)
    fetched[0].wait()
    fetched[1].wait()
    scales = jnp.transpose(stats[...].reshape(reps * 8, block))
    for r in range(reps):
        if r % per == 0:
            fetched[2 + r // per].wait()
        for k in range(slots):
            b = blocks[0, r * slots + k]
            col = scales[:, r * 8 + slots + k : r * 8 + slots + k + 1]
            for h in range(2):
                g = rows[h, r, k * block : (k + 1) * block, :].astype(F32)
                total[b, :, h * 128 : (h + 1) * 128] += g * col
            state[pl.ds(b, 1), :] += stats[r, k : k + 1, :]
    for copy in fetched[2 + groups :]:
        copy.wait()
    step = nblk // groups
    stores = []
    for i in range(groups):
        for b in range(i * step, (i + 1) * step):
            done[b] = (table[b].astype(F32) - total[b] * (1.0 / reps)).astype(BF)
        at = pl.ds(i * step, step)
        stores.append(pltpu.make_async_copy(done.at[at], table_out.at[at], sems.at[i]))
        stores[-1].start()
    accum_out[...] = accum[...] + state[...] * (1.0 / reps)
    for j in range(5):
        for h in range(2):
            dense_out[2 * j + h : 2 * j + h + 1, :] = dense[j : j + 1, h * 128 : (h + 1) * 128] * norm
    for copy in stores:
        copy.wait()


def on_device(
    pooled_cot,
    bag_ids,
    table,
    accum,
    listed_block_index,
    counts,
    x_zero,
    w_top,
    u_proj,
    v_proj,
    cross_bias,
    d_act,
):
    width = table.shape[1]
    nblk = table.shape[0] // BLOCK
    samples, feats = pooled_cot.shape[:2]
    hidden = d_act.shape[1]
    slots = listed_block_index.shape[1]
    listed_rows = slots * BLOCK
    lookups = bag_ids.shape[0]
    vmem = pl.BlockSpec(memory_space=pltpu.VMEM)
    hbm = pl.BlockSpec(memory_space=pltpu.HBM)
    dma = pltpu.SemaphoreType.DMA
    ids = jnp.transpose(bag_ids.reshape(lookups, bag_ids.shape[2]))
    state = accum.reshape(nblk, BLOCK)
    rows, stats, blocks, dense = pl.pallas_call(
        exchange,
        out_shape=(
            jax.ShapeDtypeStruct((2, NR, listed_rows, 128), BF),
            jax.ShapeDtypeStruct((NR, 8, BLOCK), F32),
            jax.ShapeDtypeStruct((1, BLOCK), jnp.int32),
            jax.ShapeDtypeStruct((8, width), F32),
        ),
        in_specs=[hbm] * 11,
        out_specs=(hbm, hbm, hbm, hbm),
        scratch_shapes=[
            pltpu.VMEM((2, NR, listed_rows, 128), BF),
            pltpu.VMEM((NR, 8, BLOCK), F32),
            pltpu.VMEM((1, BLOCK), jnp.int32),
            pltpu.VMEM((8, width), F32),
            dma((24,)),
            pltpu.VMEM(pooled_cot.shape, BF),
            pltpu.VMEM(ids.shape, jnp.int32),
            pltpu.VMEM(state.shape, F32),
            pltpu.SMEM(listed_block_index.shape, jnp.int32),
            pltpu.SMEM(counts.shape, jnp.int32),
            pltpu.VMEM(x_zero.shape, BF),
            pltpu.VMEM(w_top.shape, BF),
            pltpu.VMEM(u_proj.shape, BF),
            pltpu.VMEM(v_proj.shape, BF),
            pltpu.VMEM((1, width), F32),
            pltpu.VMEM(d_act.shape, BF),
            dma((14,)),
            pltpu.VMEM((2, samples * feats, 128), F32),
            pltpu.VMEM((2, NS, samples, 128), BF),
            pltpu.VMEM((2, NS, samples, 128), BF),
            pltpu.VMEM((listed_rows, lookups), BF),
            pltpu.VMEM((NR * samples, width), BF),
            pltpu.VMEM((NR * samples, width), BF),
            pltpu.VMEM((samples, hidden + 2 * width), BF),
            pltpu.VMEM((NR, samples, width), BF),
            pltpu.VMEM((NR, samples, width), BF),
            pltpu.VMEM((NS, 8, width), F32),
            pltpu.VMEM((NS, 8, width), F32),
            dma((2, NS)),
            dma((2, NS)),
            dma((NR,)),
            dma((NR,)),
            dma((20,)),
            dma((NR, 2)),
            dma,
            dma((2, 20)),
            dma((2, NR, 2)),
            dma((NR,)),
            dma((NR,)),
            dma((NS,)),
            dma((NS,)),
        ],
        compiler_params=pltpu.CompilerParams(
            collective_id=0, has_side_effects=True, vmem_limit_bytes=60 << 20
        ),
        name="exchange",
    )(
        pooled_cot,
        ids,
        state,
        listed_block_index,
        counts,
        x_zero,
        w_top,
        u_proj,
        v_proj,
        cross_bias.reshape(1, width),
        d_act,
    )
    total = samples * lax.axis_size("rep") * lax.axis_size("shard")
    new_table, new_accum, out = pl.pallas_call(
        functools.partial(apply, float(total) ** -0.5),
        out_shape=(
            jax.ShapeDtypeStruct((nblk, BLOCK, width), BF),
            jax.ShapeDtypeStruct((nblk, BLOCK), F32),
            jax.ShapeDtypeStruct((10, 128), F32),
        ),
        in_specs=[hbm] * 6,
        out_specs=(hbm, vmem, vmem),
        scratch_shapes=[
            pltpu.SMEM((1, BLOCK), jnp.int32),
            pltpu.VMEM((nblk, BLOCK, width), BF),
            pltpu.VMEM((nblk, BLOCK), F32),
            pltpu.VMEM((2, NR, listed_rows, 128), BF),
            pltpu.VMEM((NR, 8, BLOCK), F32),
            pltpu.VMEM((8, width), F32),
            pltpu.VMEM((nblk, BLOCK, width), BF),
            pltpu.VMEM((nblk, BLOCK, width), F32),
            pltpu.VMEM((nblk, BLOCK), F32),
            dma((4,)),
            dma((9,)),
        ],
        compiler_params=pltpu.CompilerParams(vmem_limit_bytes=60 << 20),
        name="apply",
    )(blocks, table.reshape(nblk, BLOCK, width), state, rows, stats, dense)
    return (new_table.reshape(table.shape), new_accum.reshape(accum.shape), out.reshape(1280))


def solution(mesh):
    return jax.shard_map(
        on_device,
        mesh=mesh,
        in_specs=(
            P(("rep", "shard"), None, None),
            P("rep", "shard", None),
            P("shard", None),
            P("shard"),
            P("rep", "shard"),
            P("rep", "shard"),
            P(("rep", "shard"), None),
            P(),
            P(),
            P(),
            P(),
            P(("rep", "shard"), None),
        ),
        out_specs=(P("shard", None), P("shard"), P(("rep", "shard"))),
        check_vma=False,
    )
```

time: 90.4 us -> 70.5 us (0.78)
  Pallas kernels: 79.8 us -> 69.1 us
  local copies, waits for them, and re-layouts: 8.72 us -> 0 us
    pallas_call x1, Pallas kernels: 76.3 us -> 65 us  [on_device(): pl.pallas_call(exchange, out_shape=(jax.ShapeDtypeStruct((2, NR, listed_r...]
    unnamed x22 -> x0, local copies, waits for them, and re-layouts: 8.72 us -> none
where the time goes in v2:
time: 70.5 us; the launch traced here: 70.3 us
  Pallas kernels  69.1 us (98%)
  between operations  1.29 us (2%)
    pallas_call x1, Pallas kernels, on_device(): pl.pallas_call(exchange, out_shape=(jax.ShapeDtypeStruct((2, NR, listed_r...  65 us
    pallas_call x1, Pallas kernels, on_device(): pl.pallas_call(functools.partial(apply, float(total) ** (-0.5)), out_shap...  4.03 us

profile of v2, /device:TPU:1, one launch (start us, length us, event | category | flops | bytes accessed | tf_op | source)
XLA Modules:
  0.0 70.3 jit_solution(16889606408613228620)
XLA Ops:
  1.3 65.0 %exchange.1 = (bf16[2,16,256,128]{3,2,1,0:T(8,128)(2,1)}, f32[16,8,128]{2,1,0:T(8,128)}, s32[1,128]{1,0:T(1,128)}, f32[8,256]{1,0:T(8,128)}) custom-call(bf16[64,32,256]{2,1,0:T(8,128)(2,1)} %pooled_in.1, s32[2,2048]{1,0:T(2,128)} %bitcast.12, f32[24,128]{1,0:T(8,128)} %bitcast.10, s32[1,2]{1,0:T(1,128)} %listed_in.1, s32[1,1]{1,0:T(1,128)S(6)} %copy.15.counts_in, ...), custom_call_target="tpu_custom_call" | custom-call | tf_op jit(solution)/shard_map/exchange/pallas_call | solution.py:546
  66.3 4.0 %apply.1 = (bf16[24,128,256]{2,1,0:T(8,128)(2,1)}, f32[24,128]{1,0:T(8,128)}, f32[10,128]{1,0:T(8,128)}) custom-call(s32[1,128]{1,0:T(1,128)} %get-tuple-element.10.blocks_in, bf16[24,128,256]{2,1,0:T(8,128)(2,1)} %bitcast.9, f32[24,128]{1,0:T(8,128)} %bitcast.11, bf16[2,16,256,128]{3,2,1,0:T(8,128)(2,1)} %get-tuple-element.11.rows_in, ...), custom_call_target="tpu_custom_call" | custom-call | tf_op jit(solution)/shard_map/apply/pallas_call | solution.py:617

commit v3 on v2

--- a/solution.py
+++ b/solution.py
@@ -83,6 +83,7 @@
     l_dst,
     x_dst,
     part,
+    part_src,
     part_dst,
     a_send,
     a_recv,
@@ -116,7 +117,7 @@
         (accum_in, accum),
     )
     fetched = [pltpu.make_async_copy(src, dst, in_sem.at[i]) for i, (src, dst) in enumerate(pairs)]
-    for copy in fetched:
+    for copy in fetched[:4]:
         copy.start()
 
     barrier = pltpu.get_barrier_semaphore()
@@ -219,7 +220,7 @@
 
     x_gather = Gather(x_dst, x_send, x_recv, True)
     row_gathers = (
-        Gather(rows_out.at[0], c_send.at[0], c_recv.at[0], False),
+        Gather(rows_out.at[0], c_send.at[0], c_recv.at[0], True),
         Gather(rows_out.at[1], c_send.at[1], c_recv.at[1], True, rows_hbm.at[1]),
     )
 
@@ -247,6 +248,8 @@
 
     mine, theirs = (lambda t: rep), (lambda t: t)
 
+    for copy in fetched[4:]:
+        copy.start()
     fetched[4].wait()
     x = xz[...]
     x_dst[rep] = x
@@ -363,12 +366,13 @@
 
     def spread(values, offset):
         source = lax.broadcasted_iota(jnp.int32, (width, width), 0)
-        target = lax.broadcasted_iota(jnp.int32, (width, width), 1)
-        chosen = (source == (target // 8) * 5 + target % 8 + offset) & (target % 8 < 5)
+        target = lax.broadcasted_iota(jnp.int32, (1, width), 1)
+        group, place = target >> 3, target & 7
+        chosen = source == jnp.where(place < 5, group * 5 + place + offset, -1)
         return matmul(values, jnp.where(chosen, 1.0, 0.0).astype(BF)).astype(BF)
 
     line = lax.broadcasted_iota(jnp.int32, (width, width), 0)
-    line = (line // 8) * 5 + line % 8
+    line = (line >> 3) * 5 + (line & 7)
 
     @pl.when(rep < 15)
     def _():
@@ -394,11 +398,12 @@
         above = jnp.where(rep == 14, part[...].reshape(width, width), below)
         part[...] = jnp.where(line < 64, above, below).reshape(NS, 8, width)
 
-    part_dst[shard] = part[shard]
+    part_src[...] = jnp.concatenate([part[:, :, :128], part[:, :, 128:]], axis=1).astype(BF)
+    part_dst[shard] = part_src[shard]
 
     def p_copy(p, slot):
         t = lax.rem(shard + p, NS)
-        return remote(part.at[t], part_dst.at[slot(t)], p_send.at[p], p_recv.at[slot(t)], rep, t)
+        return remote(part_src.at[t], part_dst.at[slot(t)], p_send.at[p], p_recv.at[slot(t)], rep, t)
 
     own_shard, that_shard = (lambda t: shard), (lambda t: t)
 
@@ -423,14 +428,15 @@
     blocks_out[...] = blocks.astype(jnp.int32)
     store(stats_out, stats_hbm)
     store(blocks_out, blocks_hbm)
+
+    @pl.loop(1, NS)
+    def _(p):
+        p_copy(p, that_shard).wait_recv()
+
+    dense_out[...] = jnp.sum(part_dst[...].astype(F32), axis=0)
+    store(dense_out, dense_hbm)
     row_gathers[1].end()
 
-    @pl.loop(1, NS)
-    def _(p):
-        p_copy(p, that_shard).wait_recv()
-
-    dense_out[...] = jnp.sum(part_dst[...], axis=0)
-    store(dense_out, dense_hbm)
 
     @pl.loop(1, NS)
     def _(p):
@@ -512,7 +518,7 @@
     accum_out[...] = accum[...] + state[...] * (1.0 / reps)
     for j in range(5):
         for h in range(2):
-            dense_out[2 * j + h : 2 * j + h + 1, :] = dense[j : j + 1, h * 128 : (h + 1) * 128] * norm
+            dense_out[2 * j + h : 2 * j + h + 1, :] = dense[8 * h + j : 8 * h + j + 1, :] * norm
     for copy in stores:
         copy.wait()
 
@@ -549,7 +555,7 @@
             jax.ShapeDtypeStruct((2, NR, listed_rows, 128), BF),
             jax.ShapeDtypeStruct((NR, 8, BLOCK), F32),
             jax.ShapeDtypeStruct((1, BLOCK), jnp.int32),
-            jax.ShapeDtypeStruct((8, width), F32),
+            jax.ShapeDtypeStruct((16, 128), F32),
         ),
         in_specs=[hbm] * 11,
         out_specs=(hbm, hbm, hbm, hbm),
@@ -557,7 +563,7 @@
             pltpu.VMEM((2, NR, listed_rows, 128), BF),
             pltpu.VMEM((NR, 8, BLOCK), F32),
             pltpu.VMEM((1, BLOCK), jnp.int32),
-            pltpu.VMEM((8, width), F32),
+            pltpu.VMEM((16, 128), F32),
             dma((24,)),
             pltpu.VMEM(pooled_cot.shape, BF),
             pltpu.VMEM(ids.shape, jnp.int32),
@@ -581,7 +587,8 @@
             pltpu.VMEM((NR, samples, width), BF),
             pltpu.VMEM((NR, samples, width), BF),
             pltpu.VMEM((NS, 8, width), F32),
-            pltpu.VMEM((NS, 8, width), F32),
+            pltpu.VMEM((NS, 16, 128), BF),
+            pltpu.VMEM((NS, 16, 128), BF),
             dma((2, NS)),
             dma((2, NS)),
             dma((NR,)),
@@ -629,7 +636,7 @@
             pltpu.VMEM((nblk, BLOCK), F32),
             pltpu.VMEM((2, NR, listed_rows, 128), BF),
             pltpu.VMEM((NR, 8, BLOCK), F32),
-            pltpu.VMEM((8, width), F32),
+            pltpu.VMEM((16, 128), F32),
             pltpu.VMEM((nblk, BLOCK, width), BF),
             pltpu.VMEM((nblk, BLOCK, width), F32),
             pltpu.VMEM((nblk, BLOCK), F32),

time: 70.5 us -> 69.2 us (0.982)
  Pallas kernels: 69.1 us -> 67.8 us
    pallas_call x1, Pallas kernels: 65 us -> 63.7 us  [on_device(): pl.pallas_call(exchange, out_shape=(jax.ShapeDtypeStruct((2, NR, listed_r...]
where the time goes in v3:
time: 69.2 us; the launch traced here: 69 us
  Pallas kernels  67.8 us (98%)
  between operations  1.29 us (2%)
    pallas_call x1, Pallas kernels, on_device(): pl.pallas_call(exchange, out_shape=(jax.ShapeDtypeStruct((2, NR, listed_r...  63.7 us
    pallas_call x1, Pallas kernels, on_device(): pl.pallas_call(functools.partial(apply, float(total) ** (-0.5)), out_shap...  4.03 us

profile of v3, /device:TPU:1, one launch (start us, length us, event | category | flops | bytes accessed | tf_op | source)
XLA Modules:
  0.0 69.0 jit_solution(6500020979152317820)
XLA Ops:
  1.3 63.7 %exchange.1 = (bf16[2,16,256,128]{3,2,1,0:T(8,128)(2,1)}, f32[16,8,128]{2,1,0:T(8,128)}, s32[1,128]{1,0:T(1,128)}, f32[16,128]{1,0:T(8,128)}) custom-call(bf16[64,32,256]{2,1,0:T(8,128)(2,1)} %pooled_in.1, s32[2,2048]{1,0:T(2,128)} %bitcast.12, f32[24,128]{1,0:T(8,128)} %bitcast.10, s32[1,2]{1,0:T(1,128)} %listed_in.1, s32[1,1]{1,0:T(1,128)S(6)} %copy.15.counts_in, ...), custom_call_target="tpu_custom_call" | custom-call | tf_op jit(solution)/shard_map/exchange/pallas_call | solution.py:552
  65.0 4.0 %apply.1 = (bf16[24,128,256]{2,1,0:T(8,128)(2,1)}, f32[24,128]{1,0:T(8,128)}, f32[10,128]{1,0:T(8,128)}) custom-call(s32[1,128]{1,0:T(1,128)} %get-tuple-element.10.blocks_in, bf16[24,128,256]{2,1,0:T(8,128)(2,1)} %bitcast.9, f32[24,128]{1,0:T(8,128)} %bitcast.11, bf16[2,16,256,128]{3,2,1,0:T(8,128)(2,1)} %get-tuple-element.11.rows_in, ...), custom_call_target="tpu_custom_call" | custom-call | tf_op jit(solution)/shard_map/apply/pallas_call | solution.py:624

commit v4 on v3

--- a/solution.py
+++ b/solution.py
@@ -218,10 +218,10 @@
             for copy in self.copies:
                 copy.wait_send()
 
-    x_gather = Gather(x_dst, x_send, x_recv, True)
+    x_gather = Gather(x_dst, x_send, x_recv, False)
     row_gathers = (
-        Gather(rows_out.at[0], c_send.at[0], c_recv.at[0], True),
-        Gather(rows_out.at[1], c_send.at[1], c_recv.at[1], True, rows_hbm.at[1]),
+        Gather(rows_out.at[0], c_send.at[0], c_recv.at[0], False),
+        Gather(rows_out.at[1], c_send.at[1], c_recv.at[1], False, rows_hbm.at[1]),
     )
 
     def pick(h, f):

time: 69.2 us -> 67.3 us (0.973)
  Pallas kernels: 67.8 us -> 65.9 us
    pallas_call x1, Pallas kernels: 63.7 us -> 61.8 us  [on_device(): pl.pallas_call(exchange, out_shape=(jax.ShapeDtypeStruct((2, NR, listed_r...]
where the time goes in v4:
time: 67.3 us; the launch traced here: 67.1 us
  Pallas kernels  65.9 us (98%)
  between operations  1.29 us (2%)
    pallas_call x1, Pallas kernels, on_device(): pl.pallas_call(exchange, out_shape=(jax.ShapeDtypeStruct((2, NR, listed_r...  61.8 us
    pallas_call x1, Pallas kernels, on_device(): pl.pallas_call(functools.partial(apply, float(total) ** (-0.5)), out_shap...  4.03 us

profile of v4, /device:TPU:1, one launch (start us, length us, event | category | flops | bytes accessed | tf_op | source)
XLA Modules:
  0.0 67.1 jit_solution(3185070301728475299)
XLA Ops:
  1.3 61.8 %exchange.1 = (bf16[2,16,256,128]{3,2,1,0:T(8,128)(2,1)}, f32[16,8,128]{2,1,0:T(8,128)}, s32[1,128]{1,0:T(1,128)}, f32[16,128]{1,0:T(8,128)}) custom-call(bf16[64,32,256]{2,1,0:T(8,128)(2,1)} %pooled_in.1, s32[2,2048]{1,0:T(2,128)} %bitcast.12, f32[24,128]{1,0:T(8,128)} %bitcast.10, s32[1,2]{1,0:T(1,128)} %listed_in.1, s32[1,1]{1,0:T(1,128)S(6)} %copy.15.counts_in, ...), custom_call_target="tpu_custom_call" | custom-call | tf_op jit(solution)/shard_map/exchange/pallas_call | solution.py:552
  63.1 4.0 %apply.1 = (bf16[24,128,256]{2,1,0:T(8,128)(2,1)}, f32[24,128]{1,0:T(8,128)}, f32[10,128]{1,0:T(8,128)}) custom-call(s32[1,128]{1,0:T(1,128)} %get-tuple-element.10.blocks_in, bf16[24,128,256]{2,1,0:T(8,128)(2,1)} %bitcast.9, f32[24,128]{1,0:T(8,128)} %bitcast.11, bf16[2,16,256,128]{3,2,1,0:T(8,128)(2,1)} %get-tuple-element.11.rows_in, ...), custom_call_target="tpu_custom_call" | custom-call | tf_op jit(solution)/shard_map/apply/pallas_call | solution.py:624
